TPU v7x, 128 devices: a whole 4x4x4 slice. The times are simulated.
128 devices in a mesh: ty: 8 (over x, y_hi), tx: 16 (over z, y_lo, core).
Axes of the slice: x: 4, y: 4 (y_hi: 2, y_lo: 2; y = y_hi * 2 + y_lo), z: 4, core: 2. Of those that a mesh axis runs over, the one named last changes fastest.
Arguments:
- object_slices: bfloat16 [4, 2, 2048, 4096], P(None, None, 'ty', 'tx'), may hold values from -1 to 1, as said below
- probe_wave: float32 [2, 256, 256], replicated, may hold values from -4 to 4
- intensity: float32 [384, 256, 256], P(('ty', 'tx')), may hold values from 0.1 to 4
- offsets: int32 [384, 2], P(('ty', 'tx')), may hold values from 0 to 3840, as said below
- live_slots: int32 [384], P(('ty', 'tx')), may hold values from 0 to 1, as said below
- prop_phase: float32 [256, 256], replicated, may hold values from -3.140625 to 3.140625
Outputs:
- grad_object: float32 [4, 2, 2048, 4096], P(None, None, 'ty', 'tx')
Inputs may be any that keep to these rules, and one draw needn't show every extreme that they name: `object_slices`: each complex entry has magnitude between 0.6 and 1. `offsets`: slot p belongs to device p // 3 of the mesh (ty slower, tx faster). On the device with tile (i, j) a slot's row offset lies in [i * 256 - 128, (i + 1) * 256 - 128) and its column offset in [j * 256 - 128, (j + 1) * 256 - 128), both further held within [0, 1792] and [0, 3840]; on every device both ends of each of these windows are taken by some slot. `live_slots`: on each device the live slots are its first ones, at least one; some device has all 3 live.
All inputs are finite; a program needn't handle non-finite values.
Results may differ from a plain program's by a relative error of at most 0.03.
Values may be sent and summed in bfloat16 or wider, within the bound.
A program may use at most 128 MiB of HBM per device.

v0:
```python
import math

import jax
import jax.numpy as jnp
from jax import lax
from jax.sharding import PartitionSpec as P


def passed_along(block, axis, distance):
    devices = range(lax.axis_size(axis))
    route = [(i - distance, i) for i in devices if i - distance in devices]
    return lax.ppermute(block, axis, route)


def extended(block, sides, width):
    for axis, dim in sides:
        count = lax.axis_size(axis)
        forward = [(i, i + 1) for i in range(count - 1)]
        backward = [(target, source) for source, target in forward]
        low = lax.ppermute(
            lax.slice_in_dim(block, block.shape[dim] - width, None, axis=dim), axis, forward
        )
        high = lax.ppermute(lax.slice_in_dim(block, 0, width, axis=dim), axis, backward)
        block = jnp.concatenate([low, block, high], axis=dim)
    return block


def dft_tables(probe_side):
    index = jnp.arange(probe_side, dtype=jnp.int32)
    product = index[:, None] * index[None, :] % probe_side
    angle = product.astype(jnp.float32) * (2.0 * math.pi / probe_side)
    cosine = jnp.cos(angle) / math.sqrt(probe_side)
    sine = jnp.sin(angle) / math.sqrt(probe_side)

    def block(upper):
        return jnp.stack([jnp.stack([cosine, upper], 1), jnp.stack([-upper, cosine], 1)], 0).astype(
            jnp.bfloat16
        )

    return (block(sine), block(-sine))


def transform(field, left_tab, right_tab):
    rounded = field.astype(jnp.bfloat16)
    middle = jnp.einsum(
        "aibj,bjk->aik", left_tab, rounded, preferred_element_type=jnp.float32
    ).astype(jnp.bfloat16)
    return jnp.einsum("bik,bkal->ail", middle, right_tab, preferred_element_type=jnp.float32)


def complex_mul(first, second):
    return jnp.stack(
        [first[0] * second[0] - first[1] * second[1], first[0] * second[1] + first[1] * second[0]]
    )


def exit_wave(patch_data, probe_wave, plus_tab, minus_tab, kernel):
    current = probe_wave
    slice_count = patch_data.shape[0]
    for layer in range(slice_count):
        product = complex_mul(current, patch_data[layer])
        if layer < slice_count - 1:
            spectrum = complex_mul(transform(product, plus_tab, minus_tab), kernel)
            current = transform(spectrum, minus_tab, plus_tab)
        else:
            current = transform(product, plus_tab, minus_tab)
    return current


def slot_grads(patch_data, probe_wave, measured, weight, plus_tab, minus_tab, kernel):

    def loss_of(patch_float):
        far_field = exit_wave(patch_float, probe_wave, plus_tab, minus_tab, kernel)
        power = far_field[0] * far_field[0] + far_field[1] * far_field[1]
        resid = (power - measured) * weight
        return 0.5 * jnp.sum(resid * resid)

    _, pull = jax.vjp(loss_of, patch_data.astype(jnp.float32))
    return pull(jnp.ones((), jnp.float32))[0]


def edge_rows(block, step):
    return passed_along(block, "ty", step)


def edge_cols(block, step):
    return passed_along(block, "tx", step)


def corner_move(block, row_step, col_step):
    moved = passed_along(block, "ty", row_step)
    return passed_along(moved, "tx", col_step)


def return_pieces(grad_pad, half_side, tile_rows, tile_cols):
    low_r = tile_rows + half_side
    low_c = tile_cols + half_side
    inner = grad_pad[:, :, half_side:low_r, half_side:low_c]
    inner = inner.at[:, :, tile_rows - half_side :, :].add(
        edge_rows(grad_pad[:, :, :half_side, half_side:low_c], -1)
    )
    inner = inner.at[:, :, :half_side, :].add(edge_rows(grad_pad[:, :, low_r:, half_side:low_c], 1))
    inner = inner.at[..., tile_cols - half_side :].add(
        edge_cols(grad_pad[:, :, half_side:low_r, :half_side], -1)
    )
    inner = inner.at[..., :half_side].add(edge_cols(grad_pad[:, :, half_side:low_r, low_c:], 1))
    inner = inner.at[:, :, tile_rows - half_side :, tile_cols - half_side :].add(
        corner_move(grad_pad[:, :, :half_side, :half_side], -1, -1)
    )
    inner = inner.at[:, :, tile_rows - half_side :, :half_side].add(
        corner_move(grad_pad[:, :, :half_side, low_c:], -1, 1)
    )
    inner = inner.at[:, :, :half_side, tile_cols - half_side :].add(
        corner_move(grad_pad[:, :, low_r:, :half_side], 1, -1)
    )
    inner = inner.at[:, :, :half_side, :half_side].add(
        corner_move(grad_pad[:, :, low_r:, low_c:], 1, 1)
    )
    return inner


def per_device(object_slices, probe_wave, intensity, offsets, live_slots, prop_phase):
    slice_count, _, tile_rows, tile_cols = object_slices.shape
    probe_side = probe_wave.shape[-1]
    half_side = probe_side // 2
    padded = extended(object_slices, (("ty", 2), ("tx", 3)), half_side)
    row_start = lax.axis_index("ty") * tile_rows - half_side
    col_start = lax.axis_index("tx") * tile_cols - half_side
    plus_tab, minus_tab = dft_tables(probe_side)
    kernel = jnp.stack([jnp.cos(prop_phase), jnp.sin(prop_phase)])
    grad_pad = jnp.zeros(
        (slice_count, 2, tile_rows + probe_side, tile_cols + probe_side), jnp.float32
    )
    zero_index = jnp.zeros((), jnp.int32)
    window = (slice_count, 2, probe_side, probe_side)
    for slot_index in range(offsets.shape[0]):
        start = (
            zero_index,
            zero_index,
            offsets[slot_index, 0] - row_start,
            offsets[slot_index, 1] - col_start,
        )
        patch_data = lax.dynamic_slice(padded, start, window)
        measured = intensity[slot_index]
        weight = live_slots[slot_index].astype(jnp.float32)
        grad_patch = slot_grads(
            patch_data, probe_wave, measured, weight, plus_tab, minus_tab, kernel
        )
        previous = lax.dynamic_slice(grad_pad, start, window)
        grad_pad = lax.dynamic_update_slice(grad_pad, previous + grad_patch, start)
    grad_tile = return_pieces(grad_pad, half_side, tile_rows, tile_cols)
    return grad_tile


def solution(mesh):
    in_specs = (
        P(None, None, "ty", "tx"),
        P(),
        P(("ty", "tx"), None, None),
        P(("ty", "tx"), None),
        P(("ty", "tx")),
        P(),
    )
    out_specs = P(None, None, "ty", "tx")
    return jax.shard_map(
        per_device, mesh=mesh, in_specs=in_specs, out_specs=out_specs, check_vma=False
    )
```

profile of v0, /device:TPU:43, one launch (start us, length us, event | category | flops | bytes accessed | tf_op | source)
XLA Modules:
  0.0 504.0 jit_solution(3871210166071209840)
XLA Ops:
  2.8 3.9 collective-permute-start
  6.7 3.8 collective-permute-start.1
  11.5 17.3 %collective-permute-done = bf16[4,2,128,256]{2,3,1,0:T(8,128)(2,1)S(1)} collective-permute-done((bf16[4,2,128,256]{2,3,1,0:T(8,128)(2,1)}, bf16[4,2,128,256]{2,3,1,0:T(8,128)(2,1)S(1)}, u32[]{:S(2)}, u32[]{:S(2)}) %collective-permute-start) | collective-permute-done | bytes 524320 | tf_op jit(solution)/shard_map/ppermute | solution.py:20
  28.8 3.5 collective-permute-done.1
  34.1 3.8 collective-permute-start.2
  58.7 4.2 collective-permute-done.3
  65.2 3.5 dynamic-slice_convert_fusion
  98.3 2.8 convolution_bitcast_fusion.7
  103.0 2.8 fusion.71
  108.6 2.9 fusion.73
  113.6 3.0 fusion.75
  119.2 3.0 fusion.77
  124.3 3.0 fusion.79
  130.0 3.0 fusion.81
  135.1 3.0 fusion.83
  140.4 2.9 convolution_bitcast_fusion.40
  145.1 3.0 convolution_bitcast_fusion.38
  150.1 2.9 convolution_bitcast_fusion.36
  154.7 2.9 convolution_bitcast_fusion.34
  159.5 2.8 convolution_bitcast_fusion.32
  164.2 2.8 convolution_bitcast_fusion.30
  169.0 2.8 convolution_bitcast_fusion.28
  182.2 2.9 fusion.52
  187.4 3.0 fusion.54
  193.0 2.8 convolution_bitcast_fusion.59
  200.4 2.9 fusion.56
  205.6 3.0 fusion.58
  211.4 2.8 convolution_bitcast_fusion.55
  218.8 2.9 fusion.60
  238.7 3.2 fusion.31
  244.0 2.9 fusion.33
  249.4 2.9 fusion.35
  254.4 2.9 fusion.37
  269.5 4.4 broadcast_in_dim.98
  273.9 21.5 %dynamic_update_slice.9 = f32[4,2,512,512]{2,3,1,0:T(8,128)} dynamic-update-slice(f32[4,2,512,512]{2,3,1,0:T(8,128)} %broadcast_in_dim.98, f32[4,2,256,256]{2,3,1,0:T(8,128)S(1)} %pad_add_fusion, s32[]{:T(128)} %constant.247.clone.1, s32[]{:T(128)} %constant.247.clone.1, s32[]{:T(128)S(6)} %select_n.66, s32[]{:T(128)S(6)} %select_n.67) | dynamic-update-slice | bytes 4194308 | tf_op jit(solution)/shard_map/dynamic_update_slice | solution.py:150
  300.8 19.6 %dynamic_update_slice.10 = f32[4,2,512,512]{2,3,1,0:T(8,128)} dynamic-update-slice(f32[4,2,512,512]{2,3,1,0:T(8,128)} %dynamic_update_slice.9, f32[4,2,256,256]{2,3,1,0:T(8,128)S(1)} %add_add_fusion.1, s32[]{:T(128)} %constant.247.clone.1, s32[]{:T(128)} %constant.247.clone.1, s32[]{:T(128)S(6)} %select_n.68, s32[]{:T(128)S(6)} %select_n.69) | dynamic-update-slice | bytes 4194308 | tf_op jit(solution)/shard_map/dynamic_update_slice | solution.py:150
  325.8 22.6 %dynamic_update_slice.11 = f32[4,2,512,512]{2,3,1,0:T(8,128)} dynamic-update-slice(f32[4,2,512,512]{2,3,1,0:T(8,128)} %dynamic_update_slice.10, f32[4,2,256,256]{2,3,1,0:T(8,128)S(1)} %add_add_fusion, s32[]{:T(128)} %constant.247.clone.1, s32[]{:T(128)} %constant.247.clone.1, s32[]{:T(128)S(6)} %select_n.70, s32[]{:T(128)S(6)} %select_n.71) | dynamic-update-slice | bytes 4194308 | tf_op jit(solution)/shard_map/dynamic_update_slice | solution.py:150
  350.4 5.0 collective-permute-start.4
  359.2 5.7 %collective-permute-start.8 = (f32[4,2,128,128]{2,3,1,0:T(8,128)S(1)}, f32[4,2,128,128]{2,3,1,0:T(8,128)S(1)}, u32[]{:S(2)}, u32[]{:S(2)}) collective-permute-start(f32[4,2,128,128]{2,3,1,0:T(8,128)S(1)} %get-tuple-element.104), channel_id=1, source_target_pairs={{16,0},{32,16},{48,32},{64,48},{80,64},{96,80},{112,96},{17,1},{33... | collective-permute-start | bytes 1572872 | tf_op jit(solution)/shard_map/ppermute | solution.py:12
  367.1 4.5 collective-permute-start.7
  373.2 39.4 %collective-permute-done.8 = f32[4,2,128,128]{2,3,1,0:T(8,128)S(1)} collective-permute-done((f32[4,2,128,128]{2,3,1,0:T(8,128)S(1)}, f32[4,2,128,128]{2,3,1,0:T(8,128)S(1)}, u32[]{:S(2)}, u32[]{:S(2)}) %collective-permute-start.8) | collective-permute-done | bytes 524320 | tf_op jit(solution)/shard_map/ppermute | solution.py:12
  414.5 4.9 collective-permute-start.12
  422.0 46.8 %collective-permute-done.10 = f32[4,2,128,128]{2,3,1,0:T(8,128)S(1)} collective-permute-done((f32[4,2,128,128]{2,3,1,0:T(8,128)S(1)}, f32[4,2,128,128]{2,3,1,0:T(8,128)S(1)}, u32[]{:S(2)}, u32[]{:S(2)}) %collective-permute-start.10) | collective-permute-done | bytes 524320 | tf_op jit(solution)/shard_map/ppermute | solution.py:12
  471.4 3.9 collective-permute-start.11
  477.2 4.8 collective-permute-start.15
  484.1 2.9 collective-permute-done.11
  487.2 8.0 %collective-permute-done.13 = f32[4,2,128,128]{2,3,1,0:T(8,128)S(1)} collective-permute-done((f32[4,2,128,128]{2,3,1,0:T(8,128)S(1)}, f32[4,2,128,128]{2,3,1,0:T(8,128)S(1)}, u32[]{:S(2)}, u32[]{:S(2)}) %collective-permute-start.13) | collective-permute-done | bytes 524320 | tf_op jit(solution)/shard_map/ppermute | solution.py:12
  497.4 4.3 scatter-add.36
  (213 shorter events, 182.8 us)
Async XLA Ops:
  2.8 26.0 %collective-permute-start = (bf16[4,2,128,256]{2,3,1,0:T(8,128)(2,1)}, bf16[4,2,128,256]{2,3,1,0:T(8,128)(2,1)S(1)}, u32[]{:S(2)}, u32[]{:S(2)}) collective-permute-start(bf16[4,2,128,256]{2,3,1,0:T(8,128)(2,1)} %get-tuple-element.228), channel_id=1, source_target_pairs={{0,16},{16,32},{32,48},{48,64},{64,80},{80,96},{96,112},{1,17},{17... | collective-permute-start | bytes 1572872 | tf_op jit(solution)/shard_map/ppermute | solution.py:20
  6.7 25.7 %collective-permute-start.1 = (bf16[4,2,128,256]{2,3,1,0:T(8,128)(2,1)}, bf16[4,2,128,256]{2,3,1,0:T(8,128)(2,1)S(1)}, u32[]{:S(2)}, u32[]{:S(2)}) collective-permute-start(bf16[4,2,128,256]{2,3,1,0:T(8,128)(2,1)} %get-tuple-element.229), channel_id=1, source_target_pairs={{16,0},{32,16},{48,32},{64,48},{80,64},{96,80},{112,96},{17,1},{33... | collective-permute-start | bytes 1572872 | tf_op jit(solution)/shard_map/ppermute | solution.py:23
  32.6 7.3 %copy-start.43 = (s32[3,2]{0,1:T(2,128)S(1)}, s32[3,2]{0,1:T(2,128)}, u32[]{:S(2)}) copy-start(s32[3,2]{0,1:T(2,128)} %param.25) | copy-start | bytes 76
  32.6 11.8 %copy-start.35 = (f32[256,256]{1,0:T(8,128)S(1)}, f32[256,256]{1,0:T(8,128)}, u32[]{:S(2)}) copy-start(f32[256,256]{1,0:T(8,128)} %param.27) | copy-start | bytes 786436
  32.6 12.0 %copy-start.44 = (s32[3]{0:T(128)S(1)}, s32[3]{0:T(128)}, u32[]{:S(2)}) copy-start(s32[3]{0:T(128)} %param.26) | copy-start | bytes 40
  34.1 24.6 %collective-permute-start.2 = (bf16[4,2,512,128]{2,3,1,0:T(8,128)(2,1)}, bf16[4,2,512,128]{2,3,1,0:T(8,128)(2,1)}, u32[]{:S(2)}, u32[]{:S(2)}) collective-permute-start(bf16[4,2,512,128]{2,3,1,0:T(8,128)(2,1)} %get-tuple-element.172), channel_id=1, source_target_pairs={{0,1},{1,2},{2,3},{3,4},{4,5},{5,6},{6,7},{7,8},{8,9},{9,10},{10,1... | collective-permute-start | bytes 3145736 | tf_op jit(solution)/shard_map/ppermute | solution.py:20
  37.9 25.0 %collective-permute-start.3 = (bf16[4,2,512,128]{2,3,1,0:T(8,128)(2,1)}, bf16[4,2,512,128]{2,3,1,0:T(8,128)(2,1)}, u32[]{:S(2)}, u32[]{:S(2)}) collective-permute-start(bf16[4,2,512,128]{2,3,1,0:T(8,128)(2,1)} %get-tuple-element.173), channel_id=1, source_target_pairs={{1,0},{2,1},{3,2},{4,3},{5,4},{6,5},{7,6},{8,7},{9,8},{10,9},{11,1... | collective-permute-start | bytes 3145736 | tf_op jit(solution)/shard_map/ppermute | solution.py:23
  65.2 5.6 %copy-start.36 = (bf16[1,256,2,256]{1,3,2,0:T(8,128)(2,1)S(1)}, bf16[1,256,2,256]{1,3,2,0:T(8,128)(2,1)}, u32[]{:S(2)}) copy-start(bf16[1,256,2,256]{1,3,2,0:T(8,128)(2,1)} %get-tuple-element.365) | copy-start | bytes 786436
  96.3 4.8 copy-start.34
  259.9 3.3 copy-start.37
  259.9 3.3 copy-start.38
  259.9 3.3 copy-start.39
  259.9 3.3 copy-start.40
  259.9 3.3 copy-start.41
  259.9 3.3 copy-start.42
  273.9 21.5 %copy-start.12 = (f32[1,256,256]{1,2,0:T(8,128)S(1)}, f32[1,256,256]{1,2,0:T(8,128)}, u32[]{:S(2)}) copy-start(f32[1,256,256]{1,2,0:T(8,128)} %get-tuple-element.192) | copy-start | bytes 786436
  273.9 21.5 %copy-start.13 = (f32[1,256,256]{1,2,0:T(8,128)S(1)}, f32[1,256,256]{1,2,0:T(8,128)}, u32[]{:S(2)}) copy-start(f32[1,256,256]{1,2,0:T(8,128)} %get-tuple-element.193) | copy-start | bytes 786436
  295.4 2.6 copy-start.14
  295.4 2.6 copy-start.15
  295.4 2.6 copy-start.16
  295.4 2.6 copy-start.17
  295.4 2.7 copy-start.30
  295.4 2.7 copy-start.31
  295.5 2.7 copy-start.32
  295.5 2.7 copy-start.33
  300.8 19.7 %copy-start.2 = (f32[1,256,256]{1,2,0:T(8,128)S(1)}, f32[1,256,256]{1,2,0:T(8,128)}, u32[]{:S(2)}) copy-start(f32[1,256,256]{1,2,0:T(8,128)} %get-tuple-element.175) | copy-start | bytes 786436
  300.8 19.7 %copy-start.3 = (f32[1,256,256]{1,2,0:T(8,128)S(1)}, f32[1,256,256]{1,2,0:T(8,128)}, u32[]{:S(2)}) copy-start(f32[1,256,256]{1,2,0:T(8,128)} %get-tuple-element.176) | copy-start | bytes 786436
  320.5 2.5 copy-start.5
  320.5 2.5 copy-start.6
  320.5 2.5 copy-start.7
  320.5 2.6 copy-start.8
  320.5 2.6 copy-start.9
  320.5 2.6 copy-start.10
  320.5 2.6 copy-start.11
  348.5 16.4 %copy-start = (f32[4,2,512,512]{2,3,1,0:T(8,128)S(1)}, f32[4,2,512,512]{2,3,1,0:T(8,128)}, u32[]{:S(2)}) copy-start(f32[4,2,512,512]{2,3,1,0:T(8,128)} %dynamic_update_slice.11) | copy-start | bytes 25165828
  350.4 64.2 %collective-permute-start.4 = (f32[4,2,128,256]{2,3,1,0:T(8,128)S(1)}, f32[4,2,128,256]{2,3,1,0:T(8,128)S(1)}, u32[]{:S(2)}, u32[]{:S(2)}) collective-permute-start(f32[4,2,128,256]{2,3,1,0:T(8,128)S(1)} %get-tuple-element.108), channel_id=1, source_target_pairs={{16,0},{32,16},{48,32},{64,48},{80,64},{96,80},{112,96},{17,1},{33... | collective-permute-start | bytes 3145736 | tf_op jit(solution)/shard_map/ppermute | solution.py:12
  355.4 64.0 %collective-permute-start.5 = (f32[4,2,128,256]{2,3,1,0:T(8,128)S(1)}, f32[4,2,128,256]{2,3,1,0:T(8,128)S(1)}, u32[]{:S(2)}, u32[]{:S(2)}) collective-permute-start(f32[4,2,128,256]{2,3,1,0:T(8,128)S(1)} %get-tuple-element.107), channel_id=1, source_target_pairs={{0,16},{16,32},{32,48},{48,64},{64,80},{80,96},{96,112},{1,17},{17... | collective-permute-start | bytes 3145736 | tf_op jit(solution)/shard_map/ppermute | solution.py:12
  359.2 13.0 %copy-start.45 = (s32[4]{0:T(128)S(1)}, s32[4]{0:T(128)}, u32[]{:S(2)}) copy-start(s32[4]{0:T(128)} %constant.260.clone.1) | copy-start | bytes 52
  359.2 53.4 %collective-permute-start.8 = (f32[4,2,128,128]{2,3,1,0:T(8,128)S(1)}, f32[4,2,128,128]{2,3,1,0:T(8,128)S(1)}, u32[]{:S(2)}, u32[]{:S(2)}) collective-permute-start(f32[4,2,128,128]{2,3,1,0:T(8,128)S(1)} %get-tuple-element.104), channel_id=1, source_target_pairs={{16,0},{32,16},{48,32},{64,48},{80,64},{96,80},{112,96},{17,1},{33... | collective-permute-start | bytes 1572872 | tf_op jit(solution)/shard_map/ppermute | solution.py:12
  365.1 112.1 %collective-permute-start.6 = (f32[4,2,256,128]{2,3,1,0:T(8,128)S(1)}, f32[4,2,256,128]{2,3,1,0:T(8,128)S(1)}, u32[]{:S(2)}, u32[]{:S(2)}) collective-permute-start(f32[4,2,256,128]{2,3,1,0:T(8,128)S(1)} %get-tuple-element.106), channel_id=1, source_target_pairs={{1,0},{2,1},{3,2},{4,3},{5,4},{6,5},{7,6},{8,7},{9,8},{10,9},{11,1... | collective-permute-start | bytes 3145736 | tf_op jit(solution)/shard_map/ppermute | solution.py:12
  367.1 115.2 %collective-permute-start.7 = (f32[4,2,256,128]{2,3,1,0:T(8,128)S(1)}, f32[4,2,256,128]{2,3,1,0:T(8,128)S(1)}, u32[]{:S(2)}, u32[]{:S(2)}) collective-permute-start(f32[4,2,256,128]{2,3,1,0:T(8,128)S(1)} %get-tuple-element.105), channel_id=1, source_target_pairs={{0,1},{1,2},{2,3},{3,4},{4,5},{5,6},{6,7},{7,8},{8,9},{9,10},{10,1... | collective-permute-start | bytes 3145736 | tf_op jit(solution)/shard_map/ppermute | solution.py:12
  412.6 56.2 %collective-permute-start.10 = (f32[4,2,128,128]{2,3,1,0:T(8,128)S(1)}, f32[4,2,128,128]{2,3,1,0:T(8,128)S(1)}, u32[]{:S(2)}, u32[]{:S(2)}) collective-permute-start(f32[4,2,128,128]{2,3,1,0:T(8,128)S(1)} %get-tuple-element.103), channel_id=1, source_target_pairs={{16,0},{32,16},{48,32},{64,48},{80,64},{96,80},{112,96},{17,1},{33... | collective-permute-start | bytes 1572872 | tf_op jit(solution)/shard_map/ppermute | solution.py:12
  414.5 56.9 %collective-permute-start.12 = (f32[4,2,128,128]{2,3,1,0:T(8,128)S(1)}, f32[4,2,128,128]{2,3,1,0:T(8,128)S(1)}, u32[]{:S(2)}, u32[]{:S(2)}) collective-permute-start(f32[4,2,128,128]{2,3,1,0:T(8,128)S(1)} %get-tuple-element.102), channel_id=1, source_target_pairs={{0,16},{16,32},{32,48},{48,64},{64,80},{80,96},{96,112},{1,17},{17... | collective-permute-start | bytes 1572872 | tf_op jit(solution)/shard_map/ppermute | solution.py:12
  419.4 55.8 %collective-permute-start.14 = (f32[4,2,128,128]{2,3,1,0:T(8,128)S(1)}, f32[4,2,128,128]{2,3,1,0:T(8,128)}, u32[]{:S(2)}, u32[]{:S(2)}) collective-permute-start(f32[4,2,128,128]{2,3,1,0:T(8,128)S(1)} %get-tuple-element.101), channel_id=1, source_target_pairs={{0,16},{16,32},{32,48},{48,64},{64,80},{80,96},{96,112},{1,17},{17... | collective-permute-start | bytes 1572872 | tf_op jit(solution)/shard_map/ppermute | solution.py:12
  468.8 15.2 %collective-permute-start.9 = (f32[4,2,128,128]{2,3,1,0:T(8,128)S(1)}, f32[4,2,128,128]{2,3,1,0:T(8,128)S(1)}, u32[]{:S(2)}, u32[]{:S(2)}) collective-permute-start(f32[4,2,128,128]{2,3,1,0:T(8,128)S(1)} %collective-permute-done.8), channel_id=1, source_target_pairs={{1,0},{2,1},{3,2},{4,3},{5,4},{6,5},{7,6},{8,7},{9,8},{10,9},{11,1... | collective-permute-start | bytes 1572872 | tf_op jit(solution)/shard_map/ppermute | solution.py:12
  471.4 15.7 %collective-permute-start.11 = (f32[4,2,128,128]{2,3,1,0:T(8,128)S(1)}, f32[4,2,128,128]{2,3,1,0:T(8,128)S(1)}, u32[]{:S(2)}, u32[]{:S(2)}) collective-permute-start(f32[4,2,128,128]{2,3,1,0:T(8,128)S(1)} %collective-permute-done.10), channel_id=1, source_target_pairs={{0,1},{1,2},{2,3},{3,4},{4,5},{5,6},{6,7},{7,8},{8,9},{9,10},{10,1... | collective-permute-start | bytes 1572872 | tf_op jit(solution)/shard_map/ppermute | solution.py:12
  475.3 19.9 %collective-permute-start.13 = (f32[4,2,128,128]{2,3,1,0:T(8,128)S(1)}, f32[4,2,128,128]{2,3,1,0:T(8,128)S(1)}, u32[]{:S(2)}, u32[]{:S(2)}) collective-permute-start(f32[4,2,128,128]{2,3,1,0:T(8,128)S(1)} %collective-permute-done.12), channel_id=1, source_target_pairs={{1,0},{2,1},{3,2},{4,3},{5,4},{6,5},{7,6},{8,7},{9,8},{10,9},{11,1... | collective-permute-start | bytes 1572872 | tf_op jit(solution)/shard_map/ppermute | solution.py:12
  477.2 24.5 %collective-permute-start.15 = (f32[4,2,128,128]{2,3,1,0:T(8,128)}, f32[4,2,128,128]{2,3,1,0:T(8,128)S(1)}, u32[]{:S(2)}, u32[]{:S(2)}) collective-permute-start(f32[4,2,128,128]{2,3,1,0:T(8,128)} %collective-permute-done.14), channel_id=1, source_target_pairs={{0,1},{1,2},{2,3},{3,4},{4,5},{5,6},{6,7},{7,8},{8,9},{9,10},{10,1... | collective-permute-start | bytes 1572872 | tf_op jit(solution)/shard_map/ppermute | solution.py:12
  (14 other events, 20.6 us)
where the time goes:
time: 512 us; the launch traced here: 504 us
  waiting for transfers between devices  126 us (25%)
  matrix products  118 us (23%)
  other arithmetic  104 us (20%)
  local copies, waits for them, and re-layouts  94.9 us (19%)
  starting transfers between devices  54.6 us (11%)
  between operations  6.77 us (1%)
    ppermute x12, waiting for transfers between devices, passed_along(): return lax.ppermute(block, axis, route)  98.7 us
    dynamic_update_slice x3, local copies, waits for them, and re-layouts, per_device(): grad_pad = lax.dynamic_update_slice(grad_pad, previous + grad_patch, start)  63.8 us
    dot_general x21, matrix products, transform(): jnp.einsum('bik,bkal->ail', middle, right_tab, preferred_element_type=jnp...  58.9 us
    dot_general x21, matrix products, transform(): jnp.einsum('aibj,bjk->aik', left_tab, rounded, preferred_element_type=jnp...  58.6 us
    ppermute x12, starting transfers between devices, passed_along(): return lax.ppermute(block, axis, route)  41.2 us
    mul x11, other arithmetic, complex_mul(): first[1] * second[0]  27.5 us
    another operation x15, other arithmetic  22.8 us
    ppermute x2, waiting for transfers between devices, extended(): lax.ppermute(lax.slice_in_dim(block, block.shape[dim] - width, None, axis...  19.4 us
  transfers between devices with their start and end apart: 16, of which 9 were waited for; matrix products, arithmetic and copies ran while one was open for 5% of the time, Pallas kernels for 0%

commit v1 on v0

v1 whole, which is shorter than its diff:
```python
import functools
import math

import jax
import jax.numpy as jnp
import numpy as np
from jax import lax
from jax.experimental import pallas as pl
from jax.experimental.pallas import tpu as pltpu
from jax.sharding import PartitionSpec as P

MESH = pl.DeviceIdType.MESH
BF16 = jnp.bfloat16
F32 = jnp.float32
ROWS = 32


def dft_matrix(side):
    index = np.arange(side)
    angle = (index[:, None] * index[None, :] % side) * (2.0 * math.pi / side)
    parts = np.stack([np.cos(angle), -np.sin(angle)]) / math.sqrt(side)
    return parts.astype(np.float32).astype(jnp.bfloat16).astype(np.float32)


def dot(first, second):
    return jnp.dot(first, second, preferred_element_type=F32)


def kernel(
    grid,
    off,
    live,
    obj,
    probe,
    inten,
    phase,
    dft,
    out,
    pad,
    gpad,
    patch,
    wave,
    tl,
    tle,
    tr,
    tre,
    kern,
    ub,
    mb,
    xb,
    ct,
    yb,
    zb,
    gc,
    land_r,
    land_c,
    land_d,
    land_m,
    halo_send,
    halo_recv,
    grad_send,
    grad_recv,
):
    nty, ntx = grid
    slices, _, n, _ = obj.shape
    slots = inten.shape[0]
    h = n // 2
    ty, tx = lax.axis_index("ty"), lax.axis_index("tx")
    core = lax.rem(tx, 2)
    up, down = lax.rem(ty + nty - 1, nty), lax.rem(ty + 1, nty)
    left, right = lax.rem(tx + ntx - 1, ntx), lax.rem(tx + 1, ntx)
    far = lax.rem(tx + 2 * core - 1 + ntx, ntx)
    mate = tx + 1 - 2 * core
    targets = (
        (up, tx),
        (down, tx),
        (ty, left),
        (ty, right),
        (up, far),
        (down, far),
        (ty, mate),
        (ty, mate),
    )

    def blk(index):
        return pl.ds(pl.multiple_of(index * h, h), h)

    def halo(s, d):
        top, bottom = pl.ds(0, h), pl.ds(h, h)
        low, mid, high = pl.ds(0, h), pl.ds(h, n), pl.ds(3 * h, h)
        everything = slice(None)
        src, dst = (
            (obj.at[s, :, top, :], pad.at[s, :, high, mid]),
            (obj.at[s, :, bottom, :], pad.at[s, :, low, mid]),
            (obj.at[s, :, everything, top], pad.at[s, :, mid, high]),
            (obj.at[s, :, everything, bottom], pad.at[s, :, mid, low]),
            (obj.at[s, :, top, blk(core)], pad.at[s, :, high, blk(3 * (1 - core))]),
            (obj.at[s, :, bottom, blk(core)], pad.at[s, :, low, blk(3 * (1 - core))]),
            (pad.at[s, :, low, blk(2 - core)], pad.at[s, :, low, blk(3 * core)]),
            (pad.at[s, :, high, blk(2 - core)], pad.at[s, :, high, blk(3 * core)]),
        )[d]
        return pltpu.make_async_remote_copy(
            src_ref=src,
            dst_ref=dst,
            send_sem=halo_send.at[s, d],
            recv_sem=halo_recv.at[s, d],
            device_id=targets[d],
            device_id_type=MESH,
        )

    def back(s, d):
        low, mid, high = pl.ds(0, h), pl.ds(h, n), pl.ds(3 * h, h)
        src, dst = (
            (gpad.at[s, :, low, mid], land_r.at[s, 0]),
            (gpad.at[s, :, high, mid], land_r.at[s, 1]),
            (gpad.at[s, :, mid, low], land_c.at[s, 0]),
            (gpad.at[s, :, mid, high], land_c.at[s, 1]),
            (gpad.at[s, :, low, blk(3 * core)], land_d.at[s, 0]),
            (gpad.at[s, :, high, blk(3 * core)], land_d.at[s, 1]),
            (gpad.at[s, :, low, blk(3 * (1 - core))], land_m.at[s, 0]),
            (gpad.at[s, :, high, blk(3 * (1 - core))], land_m.at[s, 1]),
        )[d]
        return pltpu.make_async_remote_copy(
            src_ref=src,
            dst_ref=dst,
            send_sem=grad_send.at[s, d],
            recv_sem=grad_recv.at[s, d],
            device_id=targets[d],
            device_id_type=MESH,
        )

    barrier = pltpu.get_barrier_semaphore()
    for target in targets[:6]:
        pl.semaphore_signal(barrier, inc=1, device_id=target, device_id_type=MESH)
    pl.semaphore_wait(barrier, 6)

    for s in range(slices):
        for d in range(6):
            halo(s, d).start()

    def corner(k):
        return off[k, 0] - (ty * n - h), off[k, 1] - (tx * n - h)

    def masks(k, r):
        a, b = corner(k)
        row = lax.broadcasted_iota(jnp.int32, (ROWS, n), 0) + r >= a
        col = lax.broadcasted_iota(jnp.int32, (ROWS, n), 1) >= b
        return row, col

    chunks = range(0, n, ROWS)

    for s in range(slices):
        pad[s, :, h : h + n, h : h + n] = obj[s]
    for r in chunks:
        kern[0, r : r + ROWS, :] = jnp.cos(phase[r : r + ROWS, :])
        kern[1, r : r + ROWS, :] = jnp.sin(phase[r : r + ROWS, :])

    def prepare(k, carry):
        a, b = corner(k)
        for axis, shift, table, sign in (
            (1, a, tl, -1.0),
            (0, a, tle, 1.0),
            (0, b, tr, 1.0),
            (1, b, tre, -1.0),
        ):
            real = pltpu.roll(dft[0], shift, axis).astype(BF16)
            imag = pltpu.roll(dft[1], shift, axis)
            table[k, 0:n, 0:n] = real
            table[k, n:, n:] = real
            table[k, 0:n, n:] = (sign * imag).astype(BF16)
            table[k, n:, 0:n] = (-sign * imag).astype(BF16)
        for part in range(2):
            moved = pltpu.roll(pltpu.roll(probe[part], a, 0), b, 1)
            wave[k, 0, :, part * n : (part + 1) * n] = moved
        return carry

    lax.fori_loop(0, slots, prepare, 0)

    def illuminate(s, k):
        for r in chunks:
            row, col = masks(k, r)
            rows = slice(r, r + ROWS)
            below = slice(n + r, n + r + ROWS)
            parts = []
            for part in range(2):
                value = jnp.where(
                    row,
                    jnp.where(col, pad[s, part, rows, 0:n].astype(F32), pad[s, part, rows, n:].astype(F32)),
                    jnp.where(col, pad[s, part, below, 0:n].astype(F32), pad[s, part, below, n:].astype(F32)),
                )
                patch[k, s, part, rows, :] = value.astype(BF16)
                parts.append(value)
            pr, pi = parts
            wr, wi = wave[k, s, rows, 0:n], wave[k, s, rows, n:]
            ub[rows, :] = (wr * pr - wi * pi).astype(BF16)
            ub[below, :] = (wr * pi + wi * pr).astype(BF16)

    def transform(left_table, right_table):
        mb[:, 0:n] = dot(left_table[0:n, :], ub[...]).astype(BF16)
        mb[:, n:] = dot(left_table[n:, :], ub[...]).astype(BF16)
        return dot(mb[...], right_table[...])

    def adjoint(k, right_table, left_table):
        yb[0:n, :] = dot(ct[k], right_table[:, 0:n]).astype(BF16)
        yb[n:, :] = dot(ct[k], right_table[:, n:]).astype(BF16)
        zb[...] = dot(left_table[...], yb[...]).astype(BF16)

    def arrive(s):
        for d in (0, 1):
            halo(s, d).wait_recv()
        for d in (6, 7):
            halo(s, d).start()
        for d in (2, 3, 4, 5, 6, 7):
            halo(s, d).wait_recv()

    def forward(s, carry):
        arrive(s)

        def slot(k, carry):
            illuminate(s, k)
            xb[...] = transform(tl.at[k], tr.at[k])
            for r in chunks:
                rows = slice(r, r + ROWS)
                below = slice(n + r, n + r + ROWS)
                kr, ki = kern[0, rows, :], kern[1, rows, :]
                xr, xi = xb[rows, 0:n], xb[rows, n:]
                ub[rows, :] = (kr * xr - ki * xi).astype(BF16)
                ub[below, :] = (kr * xi + ki * xr).astype(BF16)
            wave[k, s + 1] = transform(tle.at[k], tre.at[k])
            return carry

        return lax.fori_loop(0, slots, slot, carry)

    last = slices - 1
    lax.fori_loop(0, last, forward, 0)
    arrive(last)

    def tops(s):
        for d, rows in ((0, pl.ds(0, h)), (1, pl.ds(3 * h, h))):
            back(s, 6 + d).wait_recv()
            for part in range(2):
                place = (s, part, rows, blk(2 - core))
                total = gpad[place].astype(F32) + land_m[s, d, part].astype(F32)
                gpad[place] = total.astype(BF16)
            back(s, d).start()

    def slot_back(s, k, onward):
        adjoint(k, tre.at[k], tle.at[k])
        for r in chunks:
            rows = slice(r, r + ROWS)
            below = slice(n + r, n + r + ROWS)
            zr, zi = zb[rows, :].astype(F32), zb[below, :].astype(F32)
            wr, wi = wave[k, s, rows, 0:n], wave[k, s, rows, n:]
            gc[k, 0, rows, :] = zr * wr + zi * wi
            gc[k, 1, rows, :] = zi * wr - zr * wi
            if onward:
                pr, pi = patch[k, s, 0, rows, :].astype(F32), patch[k, s, 1, rows, :].astype(F32)
                ct[k, rows, 0:n] = (zr * pr + zi * pi).astype(BF16)
                ct[k, rows, n:] = (zi * pr - zr * pi).astype(BF16)
        if onward:
            adjoint(k, tr.at[k], tl.at[k])
            for r in chunks:
                rows = slice(r, r + ROWS)
                below = slice(n + r, n + r + ROWS)
                zr, zi = zb[rows, :].astype(F32), zb[below, :].astype(F32)
                kr, ki = kern[0, rows, :], kern[1, rows, :]
                ct[k, rows, 0:n] = (kr * zr + ki * zi).astype(BF16)
                ct[k, rows, n:] = (kr * zi - ki * zr).astype(BF16)

    def combine(s):
        for part in range(2):
            for r in chunks:
                rows = slice(r, r + ROWS)
                sums = [[None, None], [None, None]]
                for k in range(slots):
                    row, col = masks(k, r)
                    value = gc[k, part, rows, :]
                    zero = jnp.zeros_like(value)
                    for p in range(2):
                        kept = jnp.where(row, value, zero) if p == 0 else jnp.where(row, zero, value)
                        for q in range(2):
                            term = jnp.where(col, kept, zero) if q == 0 else jnp.where(col, zero, kept)
                            sums[p][q] = term if k == 0 else sums[p][q] + term
                for p in range(2):
                    start = p * n + r
                    inside = h <= start < h + n
                    for q in range(2):
                        if not inside:
                            gpad[s, part, start : start + ROWS, q * n : (q + 1) * n] = sums[p][q].astype(BF16)
                            continue
                        place = slice(start - h, start - h + ROWS)
                        if q == 0:
                            gpad[s, part, start : start + ROWS, 0:h] = sums[p][q][:, 0:h].astype(BF16)
                            out[s, part, place, 0:h] = sums[p][q][:, h:]
                        else:
                            out[s, part, place, h:] = sums[p][q][:, 0:h]
                            gpad[s, part, start : start + ROWS, 3 * h :] = sums[p][q][:, h:].astype(BF16)

    def leave(s):
        for d in (6, 7, 4, 5, 2, 3):
            back(s, d).start()

    def exit_slot(k, carry):
        illuminate(last, k)
        xb[...] = transform(tl.at[k], tr.at[k])
        weight = live[k].astype(F32)
        for r in chunks:
            rows = slice(r, r + ROWS)
            er, ei = xb[rows, 0:n], xb[rows, n:]
            resid = (er * er + ei * ei - inten[k, rows, :]) * weight
            scale = 2.0 * weight * resid
            ct[k, rows, 0:n] = (scale * er).astype(BF16)
            ct[k, rows, n:] = (scale * ei).astype(BF16)
        return carry

    lax.fori_loop(0, slots, exit_slot, 0)

    def backward(t, carry):
        s = last - t

        def slot(k, carry):
            slot_back(s, k, True)

            @pl.when((k == 0) & (t > 0))
            def _():
                tops(s + 1)

            return carry

        lax.fori_loop(0, slots, slot, 0)
        combine(s)
        leave(s)
        return carry

    lax.fori_loop(0, last, backward, 0)

    def slot_first(k, carry):
        slot_back(0, k, False)

        @pl.when(k == 0)
        def _():
            tops(1)

        return carry

    lax.fori_loop(0, slots, slot_first, 0)
    combine(0)
    leave(0)
    tops(0)

    def collect(t, carry):
        s = last - t
        for d in range(6):
            back(s, d).wait_recv()
        for part in range(2):
            out[s, part, h:, :] = out[s, part, h:, :] + land_r[s, 0, part].astype(F32)
            out[s, part, 0:h, :] = out[s, part, 0:h, :] + land_r[s, 1, part].astype(F32)
            out[s, part, :, h:] = out[s, part, :, h:] + land_c[s, 0, part].astype(F32)
            out[s, part, :, 0:h] = out[s, part, :, 0:h] + land_c[s, 1, part].astype(F32)
            for d, rows in ((0, pl.ds(h, h)), (1, pl.ds(0, h))):
                place = (s, part, rows, blk(core))
                out[place] = out[place] + land_d[s, d, part].astype(F32)
        return carry

    lax.fori_loop(0, slices, collect, 0)

    def drain(s, carry):
        for d in range(8):
            halo(s, d).wait_send()
            back(s, d).wait_send()
        return carry

    lax.fori_loop(0, slices, drain, 0)


def per_device(grid, object_slices, probe_wave, intensity, offsets, live_slots, prop_phase):
    slices, _, n, _ = object_slices.shape
    slots = intensity.shape[0]
    h = n // 2
    vmem, smem = pl.BlockSpec(memory_space=pltpu.VMEM), pl.BlockSpec(memory_space=pltpu.SMEM)
    table = pltpu.VMEM((slots, 2 * n, 2 * n), BF16)
    return pl.pallas_call(
        functools.partial(kernel, grid),
        out_shape=jax.ShapeDtypeStruct(object_slices.shape, F32),
        in_specs=[smem, smem, vmem, vmem, vmem, vmem, vmem],
        out_specs=vmem,
        scratch_shapes=[
            pltpu.VMEM((slices, 2, 2 * n, 2 * n), BF16),
            pltpu.VMEM((slices, 2, 2 * n, 2 * n), BF16),
            pltpu.VMEM((slots, slices, 2, n, n), BF16),
            pltpu.VMEM((slots, slices, n, 2 * n), F32),
            table,
            table,
            table,
            table,
            pltpu.VMEM((2, n, n), F32),
            pltpu.VMEM((2 * n, n), BF16),
            pltpu.VMEM((n, 2 * n), BF16),
            pltpu.VMEM((n, 2 * n), F32),
            pltpu.VMEM((slots, n, 2 * n), BF16),
            pltpu.VMEM((2 * n, n), BF16),
            pltpu.VMEM((2 * n, n), BF16),
            pltpu.VMEM((slots, 2, n, n), F32),
            pltpu.VMEM((slices, 2, 2, h, n), BF16),
            pltpu.VMEM((slices, 2, 2, n, h), BF16),
            pltpu.VMEM((slices, 2, 2, h, h), BF16),
            pltpu.VMEM((slices, 2, 2, h, h), BF16),
            pltpu.SemaphoreType.DMA((slices, 8)),
            pltpu.SemaphoreType.DMA((slices, 8)),
            pltpu.SemaphoreType.DMA((slices, 8)),
            pltpu.SemaphoreType.DMA((slices, 8)),
        ],
        compiler_params=pltpu.CompilerParams(
            collective_id=0, has_side_effects=True, vmem_limit_bytes=56 * 1024 * 1024
        ),
    )(
        offsets,
        live_slots,
        object_slices,
        probe_wave,
        intensity,
        prop_phase,
        jnp.asarray(dft_matrix(n)),
    )


def solution(mesh):
    in_specs = (
        P(None, None, "ty", "tx"),
        P(),
        P(("ty", "tx"), None, None),
        P(("ty", "tx"), None),
        P(("ty", "tx")),
        P(),
    )
    out_specs = P(None, None, "ty", "tx")
    grid = (mesh.shape["ty"], mesh.shape["tx"])
    return jax.shard_map(
        functools.partial(per_device, grid),
        mesh=mesh,
        in_specs=in_specs,
        out_specs=out_specs,
        check_vma=False,
    )
```

time: 512 us -> 102 us (0.20)
  the two profiles are of different devices: /device:TPU:43 before, /device:TPU:1 now
where the time goes in v1:
time: 102 us
  Pallas kernels  97.7 us (96%)
  local copies, waits for them, and re-layouts  4.38 us (4%)
    pallas_call x1, Pallas kernels, per_device(): pl.pallas_call(functools.partial(kernel, grid), out_shape=jax.ShapeDtypeS...  97.7 us
    unnamed x2, local copies, waits for them, and re-layouts  4.38 us

profile of v1, /device:TPU:1, one launch (start us, length us, event | category | flops | bytes accessed | tf_op | source)
XLA Modules:
  0.0 102.1 jit_solution(8392057567278379162)
XLA Ops:
  0.0 1.3 %copy.8.off = s32[3,2]{1,0:T(4,128)} copy(s32[3,2]{0,1:T(2,128)} %param.10) | data formatting | bytes 48 | tf_op args[3]
  1.3 97.7 %shard_map.73 = f32[4,2,256,256]{3,2,1,0:T(8,128)} custom-call(s32[3,2]{1,0:T(4,128)} %copy.8.off, s32[3]{0:T(128)} %live.1, bf16[4,2,256,256]{3,2,1,0:T(8,128)(2,1)} %obj.1, f32[2,256,256]{2,1,0:T(8,128)} %probe.1, f32[3,256,256]{2,1,0:T(8,128)} %inten.1, f32[256,256]{1,0:T(8,128)} %phase.1, f32[2,256,256]{2,1,0:T(8,128)} %constant.2.clone.dft), custom_call_target="tpu_custom_call" | custom-call | tf_op jit(solution)/shard_map/pallas_call | solution.py:382
  99.1 3.0 %copy.10 = f32[4,2,256,256]{3,2,1,0:T(8,128)} copy(f32[4,2,256,256]{3,2,1,0:T(8,128)} %shard_map.73) | data formatting | bytes 4194304

commit v2 on v1

v2 whole, which is shorter than its diff:
```python
import functools
import math

import jax
import jax.numpy as jnp
import numpy as np
from jax import lax
from jax.experimental import pallas as pl
from jax.experimental.pallas import tpu as pltpu
from jax.sharding import PartitionSpec as P

MESH = pl.DeviceIdType.MESH
BF16 = jnp.bfloat16
F32 = jnp.float32
ROWS = 32


def dft_matrix(side):
    index = np.arange(side)
    angle = (index[:, None] * index[None, :] % side) * (2.0 * math.pi / side)
    parts = np.stack([np.cos(angle), -np.sin(angle)]) / math.sqrt(side)
    return parts.astype(np.float32).astype(jnp.bfloat16).astype(np.float32)


def dot(first, second):
    return jnp.dot(first, second, preferred_element_type=F32)


def kernel(
    grid,
    off,
    live,
    obj,
    probe_in,
    inten_in,
    phase_in,
    dft_in,
    out,
    probe,
    inten,
    phase,
    dft,
    pad,
    gpad,
    patch,
    wave,
    tl,
    tle,
    tr,
    tre,
    kern,
    ub,
    mb,
    xb,
    ct,
    yb,
    zb,
    gc,
    land_r,
    land_c,
    land_d,
    land_m,
    halo_send,
    halo_recv,
    grad_send,
    grad_recv,
    own_sem,
):
    nty, ntx = grid
    slices, _, n, _ = obj.shape
    slots = inten.shape[0]
    h = n // 2
    ty, tx = lax.axis_index("ty"), lax.axis_index("tx")
    core = lax.rem(tx, 2)
    up, down = lax.rem(ty + nty - 1, nty), lax.rem(ty + 1, nty)
    left, right = lax.rem(tx + ntx - 1, ntx), lax.rem(tx + 1, ntx)
    far = lax.rem(tx + 2 * core - 1 + ntx, ntx)
    mate = tx + 1 - 2 * core
    targets = (
        (up, tx),
        (up, tx),
        (down, tx),
        (down, tx),
        (ty, left),
        (ty, right),
        (up, far),
        (down, far),
        (ty, mate),
        (ty, mate),
    )
    low, mid, high = pl.ds(0, h), pl.ds(h, n), pl.ds(3 * h, h)

    def blk(index):
        return pl.ds(pl.multiple_of(index * h, h), h)

    def remote(src, dst, send_sem, recv_sem, target):
        return pltpu.make_async_remote_copy(
            src_ref=src,
            dst_ref=dst,
            send_sem=send_sem,
            recv_sem=recv_sem,
            device_id=target,
            device_id_type=MESH,
        )

    def halo(s, d):
        top, bottom = pl.ds(0, h), pl.ds(h, h)
        everything = slice(None)
        near, away = 1 - core, core
        src, dst = (
            (obj.at[s, :, top, blk(near)], pad.at[s, :, high, blk(1 + near)]),
            (obj.at[s, :, top, blk(away)], pad.at[s, :, high, blk(1 + away)]),
            (obj.at[s, :, bottom, blk(near)], pad.at[s, :, low, blk(1 + near)]),
            (obj.at[s, :, bottom, blk(away)], pad.at[s, :, low, blk(1 + away)]),
            (obj.at[s, :, everything, top], pad.at[s, :, mid, high]),
            (obj.at[s, :, everything, bottom], pad.at[s, :, mid, low]),
            (obj.at[s, :, top, blk(core)], pad.at[s, :, high, blk(3 * (1 - core))]),
            (obj.at[s, :, bottom, blk(core)], pad.at[s, :, low, blk(3 * (1 - core))]),
            (pad.at[s, :, low, blk(1 + near)], pad.at[s, :, low, blk(3 * core)]),
            (pad.at[s, :, high, blk(1 + near)], pad.at[s, :, high, blk(3 * core)]),
        )[d]
        return remote(src, dst, halo_send.at[s, d], halo_recv.at[s, d], targets[d])

    def back(s, d):
        near, away = 1 - core, core
        src, dst = (
            (gpad.at[s, :, low, blk(1 + near)], land_r.at[s, 0, :, :, blk(near)]),
            (gpad.at[s, :, low, blk(1 + away)], land_r.at[s, 0, :, :, blk(away)]),
            (gpad.at[s, :, high, blk(1 + near)], land_r.at[s, 1, :, :, blk(near)]),
            (gpad.at[s, :, high, blk(1 + away)], land_r.at[s, 1, :, :, blk(away)]),
            (gpad.at[s, :, mid, low], land_c.at[s, 0]),
            (gpad.at[s, :, mid, high], land_c.at[s, 1]),
            (gpad.at[s, :, low, blk(3 * core)], land_d.at[s, 0]),
            (gpad.at[s, :, high, blk(3 * core)], land_d.at[s, 1]),
            (gpad.at[s, :, low, blk(3 * (1 - core))], land_m.at[s, 0]),
            (gpad.at[s, :, high, blk(3 * (1 - core))], land_m.at[s, 1]),
        )[d]
        return remote(src, dst, grad_send.at[s, d], grad_recv.at[s, d], targets[d])

    own = [
        pltpu.make_async_copy(src, dst, own_sem.at[index])
        for index, (src, dst) in enumerate(
            ((dft_in, dft), (probe_in, probe), (phase_in, phase), (obj, pad.at[:, :, mid, mid]), (inten_in, inten))
        )
    ]

    barrier = pltpu.get_barrier_semaphore()
    for target in ((up, tx), (down, tx), (ty, left), (ty, right), (up, far), (down, far)):
        pl.semaphore_signal(barrier, inc=1, device_id=target, device_id_type=MESH)
    pl.semaphore_wait(barrier, 6)

    for s in range(slices):
        for d in (4, 5):
            halo(s, d).start()
    for s in range(slices):
        for d in (6, 7, 0, 2, 1, 3):
            halo(s, d).start()
    for copy in own:
        copy.start()

    def corner(k):
        return off[0, k] - (ty * n - h), off[1, k] - (tx * n - h)

    def masks(k, r):
        a, b = corner(k)
        row = lax.broadcasted_iota(jnp.int32, (ROWS, n), 0) + r >= a
        col = lax.broadcasted_iota(jnp.int32, (ROWS, n), 1) >= b
        return row, col

    chunks = range(0, n, ROWS)

    for copy in own[:3]:
        copy.wait()
    for r in chunks:
        kern[0, r : r + ROWS, :] = jnp.cos(phase[r : r + ROWS, :])
        kern[1, r : r + ROWS, :] = jnp.sin(phase[r : r + ROWS, :])

    def prepare(k, carry):
        a, b = corner(k)
        for axis, shift, table, sign in (
            (1, a, tl, -1.0),
            (0, a, tle, 1.0),
            (0, b, tr, 1.0),
            (1, b, tre, -1.0),
        ):
            real = pltpu.roll(dft[0], shift, axis).astype(BF16)
            imag = pltpu.roll(dft[1], shift, axis)
            table[k, 0:n, 0:n] = real
            table[k, n:, n:] = real
            table[k, 0:n, n:] = (sign * imag).astype(BF16)
            table[k, n:, 0:n] = (-sign * imag).astype(BF16)
        for part in range(2):
            moved = pltpu.roll(pltpu.roll(probe[part], a, 0), b, 1)
            wave[k, 0, :, part * n : (part + 1) * n] = moved
        return carry

    lax.fori_loop(0, slots, prepare, 0)
    for copy in own[3:]:
        copy.wait()

    def illuminate(s, k):
        for r in chunks:
            row, col = masks(k, r)
            rows = slice(r, r + ROWS)
            below = slice(n + r, n + r + ROWS)
            parts = []
            for part in range(2):
                value = jnp.where(
                    row,
                    jnp.where(col, pad[s, part, rows, 0:n].astype(F32), pad[s, part, rows, n:].astype(F32)),
                    jnp.where(col, pad[s, part, below, 0:n].astype(F32), pad[s, part, below, n:].astype(F32)),
                )
                patch[k, s, part, rows, :] = value.astype(BF16)
                parts.append(value)
            pr, pi = parts
            wr, wi = wave[k, s, rows, 0:n], wave[k, s, rows, n:]
            ub[k, rows, :] = (wr * pr - wi * pi).astype(BF16)
            ub[k, below, :] = (wr * pi + wi * pr).astype(BF16)

    def left_of(k, table):
        mb[k, :, 0:n] = dot(table[k, 0:n, :], ub[k]).astype(BF16)
        mb[k, :, n:] = dot(table[k, n:, :], ub[k]).astype(BF16)

    def propagate(k):
        for r in chunks:
            rows = slice(r, r + ROWS)
            below = slice(n + r, n + r + ROWS)
            kr, ki = kern[0, rows, :], kern[1, rows, :]
            xr, xi = xb[k, rows, 0:n], xb[k, rows, n:]
            ub[k, rows, :] = (kr * xr - ki * xi).astype(BF16)
            ub[k, below, :] = (kr * xi + ki * xr).astype(BF16)

    def residual(k):
        weight = live[k].astype(F32)
        for r in chunks:
            rows = slice(r, r + ROWS)
            er, ei = xb[k, rows, 0:n], xb[k, rows, n:]
            resid = (er * er + ei * ei - inten[k, rows, :]) * weight
            scale = 2.0 * weight * resid
            ct[k, rows, 0:n] = (scale * er).astype(BF16)
            ct[k, rows, n:] = (scale * ei).astype(BF16)

    def right_adjoint(k, table):
        yb[k, 0:n, :] = dot(ct[k], table[k, :, 0:n]).astype(BF16)
        yb[k, n:, :] = dot(ct[k], table[k, :, n:]).astype(BF16)

    def left_adjoint(k, table):
        zb[k] = dot(table[k], yb[k]).astype(BF16)

    def gradient(s, k, onward):
        for r in chunks:
            rows = slice(r, r + ROWS)
            below = slice(n + r, n + r + ROWS)
            zr, zi = zb[k, rows, :].astype(F32), zb[k, below, :].astype(F32)
            wr, wi = wave[k, s, rows, 0:n], wave[k, s, rows, n:]
            gc[k, 0, rows, :] = zr * wr + zi * wi
            gc[k, 1, rows, :] = zi * wr - zr * wi
            if onward:
                pr, pi = patch[k, s, 0, rows, :].astype(F32), patch[k, s, 1, rows, :].astype(F32)
                ct[k, rows, 0:n] = (zr * pr + zi * pi).astype(BF16)
                ct[k, rows, n:] = (zi * pr - zr * pi).astype(BF16)

    def propagate_adjoint(k):
        for r in chunks:
            rows = slice(r, r + ROWS)
            below = slice(n + r, n + r + ROWS)
            zr, zi = zb[k, rows, :].astype(F32), zb[k, below, :].astype(F32)
            kr, ki = kern[0, rows, :], kern[1, rows, :]
            ct[k, rows, 0:n] = (kr * zr + ki * zi).astype(BF16)
            ct[k, rows, n:] = (kr * zi - ki * zr).astype(BF16)

    def every(stage, *operands):
        for k in range(slots):
            stage(k, *operands)

    def arrive(s):
        for d in (0, 2):
            halo(s, d).wait_recv()
        for d in (8, 9):
            halo(s, d).start()
        for d in (1, 3, 4, 5, 6, 7, 8, 9):
            halo(s, d).wait_recv()

    def forward(s, carry):
        arrive(s)
        for k in range(slots):
            illuminate(s, k)
        every(left_of, tl)
        for k in range(slots):
            xb[k] = dot(mb[k], tr[k])
        every(propagate)
        every(left_of, tle)
        for k in range(slots):
            wave[k, s + 1] = dot(mb[k], tre[k])
        return carry

    last = slices - 1
    lax.fori_loop(0, last, forward, 0)
    arrive(last)

    def tops(s):
        for d, rows in ((0, pl.ds(0, h)), (1, pl.ds(3 * h, h))):
            back(s, 8 + d).wait_recv()
            for part in range(2):
                place = (s, part, rows, blk(2 - core))
                total = gpad[place].astype(F32) + land_m[s, d, part].astype(F32)
                gpad[place] = total.astype(BF16)
            back(s, 2 * d).start()

    def combine(s):
        for part in range(2):
            for r in chunks:
                rows = slice(r, r + ROWS)
                sums = [[None, None], [None, None]]
                for k in range(slots):
                    row, col = masks(k, r)
                    value = gc[k, part, rows, :]
                    zero = jnp.zeros_like(value)
                    for p in range(2):
                        kept = jnp.where(row, value, zero) if p == 0 else jnp.where(row, zero, value)
                        for q in range(2):
                            term = jnp.where(col, kept, zero) if q == 0 else jnp.where(col, zero, kept)
                            sums[p][q] = term if k == 0 else sums[p][q] + term
                for p in range(2):
                    start = p * n + r
                    inside = h <= start < h + n
                    for q in range(2):
                        if not inside:
                            gpad[s, part, start : start + ROWS, q * n : (q + 1) * n] = sums[p][q].astype(BF16)
                            continue
                        place = slice(start - h, start - h + ROWS)
                        if q == 0:
                            gpad[s, part, start : start + ROWS, 0:h] = sums[p][q][:, 0:h].astype(BF16)
                            out[s, part, place, 0:h] = sums[p][q][:, h:]
                        else:
                            out[s, part, place, h:] = sums[p][q][:, 0:h]
                            gpad[s, part, start : start + ROWS, 3 * h :] = sums[p][q][:, h:].astype(BF16)

    def leave(s):
        for d in (8, 9, 4, 5, 6, 7, 1, 3):
            back(s, d).start()

    for k in range(slots):
        illuminate(last, k)
    every(left_of, tl)
    for k in range(slots):
        xb[k] = dot(mb[k], tr[k])
    every(residual)

    def backward(t, carry):
        s = last - t
        every(right_adjoint, tre)
        every(left_adjoint, tle)

        @pl.when(t > 0)
        def _():
            tops(s + 1)

        for k in range(slots):
            gradient(s, k, True)
        combine(s)
        leave(s)
        every(right_adjoint, tr)
        every(left_adjoint, tl)
        every(propagate_adjoint)
        return carry

    lax.fori_loop(0, last, backward, 0)
    every(right_adjoint, tre)
    every(left_adjoint, tle)
    tops(1)
    for k in range(slots):
        gradient(0, k, False)
    combine(0)
    leave(0)
    tops(0)

    def collect(t, carry):
        s = last - t
        for d in range(8):
            back(s, d).wait_recv()
        for part in range(2):
            out[s, part, h:, :] = out[s, part, h:, :] + land_r[s, 0, part].astype(F32)
            out[s, part, 0:h, :] = out[s, part, 0:h, :] + land_r[s, 1, part].astype(F32)
            out[s, part, :, h:] = out[s, part, :, h:] + land_c[s, 0, part].astype(F32)
            out[s, part, :, 0:h] = out[s, part, :, 0:h] + land_c[s, 1, part].astype(F32)
            for d, rows in ((0, pl.ds(h, h)), (1, pl.ds(0, h))):
                place = (s, part, rows, blk(core))
                out[place] = out[place] + land_d[s, d, part].astype(F32)
        return carry

    lax.fori_loop(0, slices, collect, 0)

    def drain(s, carry):
        for d in range(10):
            halo(s, d).wait_send()
            back(s, d).wait_send()
        return carry

    lax.fori_loop(0, slices, drain, 0)


def per_device(grid, object_slices, probe_wave, intensity, offsets, live_slots, prop_phase):
    slices, _, n, _ = object_slices.shape
    slots = intensity.shape[0]
    h = n // 2
    vmem, smem = pl.BlockSpec(memory_space=pltpu.VMEM), pl.BlockSpec(memory_space=pltpu.SMEM)
    table = pltpu.VMEM((slots, 2 * n, 2 * n), BF16)
    return pl.pallas_call(
        functools.partial(kernel, grid),
        out_shape=pltpu.VMEM(object_slices.shape, F32),
        in_specs=[smem, smem] + [pl.BlockSpec(memory_space=pl.ANY)] * 5,
        out_specs=vmem,
        scratch_shapes=[
            pltpu.VMEM(probe_wave.shape, F32),
            pltpu.VMEM(intensity.shape, F32),
            pltpu.VMEM(prop_phase.shape, F32),
            pltpu.VMEM((2, n, n), F32),
            pltpu.VMEM((slices, 2, 2 * n, 2 * n), BF16),
            pltpu.VMEM((slices, 2, 2 * n, 2 * n), BF16),
            pltpu.VMEM((slots, slices, 2, n, n), BF16),
            pltpu.VMEM((slots, slices, n, 2 * n), F32),
            table,
            table,
            table,
            table,
            pltpu.VMEM((2, n, n), F32),
            pltpu.VMEM((slots, 2 * n, n), BF16),
            pltpu.VMEM((slots, n, 2 * n), BF16),
            pltpu.VMEM((slots, n, 2 * n), F32),
            pltpu.VMEM((slots, n, 2 * n), BF16),
            pltpu.VMEM((slots, 2 * n, n), BF16),
            pltpu.VMEM((slots, 2 * n, n), BF16),
            pltpu.VMEM((slots, 2, n, n), F32),
            pltpu.VMEM((slices, 2, 2, h, n), BF16),
            pltpu.VMEM((slices, 2, 2, n, h), BF16),
            pltpu.VMEM((slices, 2, 2, h, h), BF16),
            pltpu.VMEM((slices, 2, 2, h, h), BF16),
            pltpu.SemaphoreType.DMA((slices, 10)),
            pltpu.SemaphoreType.DMA((slices, 10)),
            pltpu.SemaphoreType.DMA((slices, 10)),
            pltpu.SemaphoreType.DMA((slices, 10)),
            pltpu.SemaphoreType.DMA((5,)),
        ],
        compiler_params=pltpu.CompilerParams(
            collective_id=0, has_side_effects=True, vmem_limit_bytes=56 * 1024 * 1024
        ),
    )(
        offsets.T,
        live_slots,
        object_slices,
        probe_wave,
        intensity,
        prop_phase,
        jnp.asarray(dft_matrix(n)),
    )


def solution(mesh):
    in_specs = (
        P(None, None, "ty", "tx"),
        P(),
        P(("ty", "tx"), None, None),
        P(("ty", "tx"), None),
        P(("ty", "tx")),
        P(),
    )
    out_specs = P(None, None, "ty", "tx")
    grid = (mesh.shape["ty"], mesh.shape["tx"])
    return jax.shard_map(
        functools.partial(per_device, grid),
        mesh=mesh,
        in_specs=in_specs,
        out_specs=out_specs,
        check_vma=False,
    )
```

time: 102 us -> 93.3 us (0.915)
  Pallas kernels: 97.7 us -> 91.8 us
  local copies, waits for them, and re-layouts: 4.38 us -> 1.32 us
    pallas_call x1, Pallas kernels: 97.7 us -> 91.8 us  [per_device(): pl.pallas_call(functools.partial(kernel, grid), out_shape=pltpu.VMEM(obje...]
    unnamed x2 -> x1, local copies, waits for them, and re-layouts: 4.38 us -> 1.32 us
where the time goes in v2:
time: 93.3 us; the launch traced here: 93.1 us
  Pallas kernels  91.8 us (98%)
  local copies, waits for them, and re-layouts  1.32 us (1%)
    pallas_call x1, Pallas kernels, per_device(): pl.pallas_call(functools.partial(kernel, grid), out_shape=pltpu.VMEM(obje...  91.8 us

profile of v2, /device:TPU:1, one launch (start us, length us, event | category | flops | bytes accessed | tf_op | source)
XLA Modules:
  0.0 93.1 jit_solution(2390462750506462748)
XLA Ops:
  0.0 91.8 %shard_map.73 = f32[4,2,256,256]{3,2,1,0:T(8,128)S(1)} custom-call(s32[2,3]{1,0:T(2,128)} %bitcast.1, s32[3]{0:T(128)} %live.1, bf16[4,2,256,256]{3,2,1,0:T(8,128)(2,1)} %obj.1, f32[2,256,256]{2,1,0:T(8,128)} %probe_in.1, f32[3,256,256]{2,1,0:T(8,128)} %inten_in.1, f32[256,256]{1,0:T(8,128)} %phase_in.1, f32[2,256,256]{2,1,0:T(8,128)} %constant.2.clone.dft_in), custom_call_target="tpu_custom_call" | custom-call | tf_op jit(solution)/shard_map/pallas_call | solution.py:409
  91.8 1.3 %copy.9 = f32[4,2,256,256]{3,2,1,0:T(8,128)} copy(f32[4,2,256,256]{3,2,1,0:T(8,128)S(1)} %shard_map.73) | data formatting | bytes 4194304

commit v3 on v2

--- a/solution.py
+++ b/solution.py
@@ -88,6 +88,45 @@
         (ty, mate),
         (ty, mate),
     )
+    has_up, has_down, has_left, has_right = ty > 0, ty < nty - 1, tx > 0, tx < ntx - 1
+    has_far = ((core == 0) & has_left) | ((core == 1) & has_right)
+    sends = (
+        has_up,
+        has_up,
+        has_down,
+        has_down,
+        has_left,
+        has_right,
+        has_up & has_far,
+        has_down & has_far,
+        has_up,
+        has_down,
+    )
+    gets = (
+        has_down,
+        has_down,
+        has_up,
+        has_up,
+        has_right,
+        has_left,
+        has_down & has_far,
+        has_up & has_far,
+        has_up,
+        has_down,
+    )
+
+    def start(way, s, ds):
+        for d in ds:
+            pl.when(sends[d])(way(s, d).start)
+
+    def await_arrival(way, s, ds):
+        for d in ds:
+            pl.when(gets[d])(way(s, d).wait_recv)
+
+    def await_departure(way, s, ds):
+        for d in ds:
+            pl.when(sends[d])(way(s, d).wait_send)
+
     low, mid, high = pl.ds(0, h), pl.ds(h, n), pl.ds(3 * h, h)
 
     def blk(index):
@@ -145,16 +184,18 @@
     ]
 
     barrier = pltpu.get_barrier_semaphore()
-    for target in ((up, tx), (down, tx), (ty, left), (ty, right), (up, far), (down, far)):
-        pl.semaphore_signal(barrier, inc=1, device_id=target, device_id_type=MESH)
-    pl.semaphore_wait(barrier, 6)
+    for d in (0, 2, 4, 5, 6, 7):
+
+        @pl.when(sends[d])
+        def _(d=d):
+            pl.semaphore_signal(barrier, inc=1, device_id=targets[d], device_id_type=MESH)
+
+    pl.semaphore_wait(barrier, sum(sends[d].astype(jnp.int32) for d in (0, 2, 4, 5, 6, 7)))
 
     for s in range(slices):
-        for d in (4, 5):
-            halo(s, d).start()
+        start(halo, s, (4, 5))
     for s in range(slices):
-        for d in (6, 7, 0, 2, 1, 3):
-            halo(s, d).start()
+        start(halo, s, (6, 7, 0, 2, 1, 3))
     for copy in own:
         copy.start()
 
@@ -274,12 +315,9 @@
             stage(k, *operands)
 
     def arrive(s):
-        for d in (0, 2):
-            halo(s, d).wait_recv()
-        for d in (8, 9):
-            halo(s, d).start()
-        for d in (1, 3, 4, 5, 6, 7, 8, 9):
-            halo(s, d).wait_recv()
+        await_arrival(halo, s, (0, 2))
+        start(halo, s, (8, 9))
+        await_arrival(halo, s, (1, 3, 4, 5, 6, 7, 8, 9))
 
     def forward(s, carry):
         arrive(s)
@@ -299,13 +337,16 @@
     arrive(last)
 
     def tops(s):
-        for d, rows in ((0, pl.ds(0, h)), (1, pl.ds(3 * h, h))):
-            back(s, 8 + d).wait_recv()
-            for part in range(2):
-                place = (s, part, rows, blk(2 - core))
-                total = gpad[place].astype(F32) + land_m[s, d, part].astype(F32)
-                gpad[place] = total.astype(BF16)
-            back(s, 2 * d).start()
+        for d, rows in ((0, low), (1, high)):
+
+            @pl.when(gets[8 + d])
+            def _(d=d, rows=rows):
+                back(s, 8 + d).wait_recv()
+                for part in range(2):
+                    place = (s, part, rows, blk(2 - core))
+                    total = gpad[place].astype(F32) + land_m[s, d, part].astype(F32)
+                    gpad[place] = total.astype(BF16)
+                back(s, 2 * d).start()
 
     def combine(s):
         for part in range(2):
@@ -336,9 +377,12 @@
                             out[s, part, place, h:] = sums[p][q][:, 0:h]
                             gpad[s, part, start : start + ROWS, 3 * h :] = sums[p][q][:, h:].astype(BF16)
 
-    def leave(s):
-        for d in (8, 9, 4, 5, 6, 7, 1, 3):
-            back(s, d).start()
+    def sides(s):
+        start(back, s, (8, 9, 4, 5, 6, 7))
+
+    def rows_out(s):
+        start(back, s, (1, 3))
+        tops(s)
 
     for k in range(slots):
         illuminate(last, k)
@@ -351,16 +395,25 @@
         s = last - t
         every(right_adjoint, tre)
         every(left_adjoint, tle)
-
-        @pl.when(t > 0)
-        def _():
-            tops(s + 1)
-
         for k in range(slots):
             gradient(s, k, True)
         combine(s)
-        leave(s)
+        sides(s)
+
+        @pl.when(t > 1)
+        def _():
+            rows_out(s + 1)
+
+        @pl.when(t == 0)
+        def _():
+            start(back, s, (1, 3))
+
         every(right_adjoint, tr)
+
+        @pl.when(t == 0)
+        def _():
+            tops(s)
+
         every(left_adjoint, tl)
         every(propagate_adjoint)
         return carry
@@ -368,33 +421,40 @@
     lax.fori_loop(0, last, backward, 0)
     every(right_adjoint, tre)
     every(left_adjoint, tle)
-    tops(1)
     for k in range(slots):
         gradient(0, k, False)
     combine(0)
-    leave(0)
-    tops(0)
+    sides(0)
+    rows_out(1)
+    rows_out(0)
 
     def collect(t, carry):
         s = last - t
-        for d in range(8):
-            back(s, d).wait_recv()
-        for part in range(2):
-            out[s, part, h:, :] = out[s, part, h:, :] + land_r[s, 0, part].astype(F32)
-            out[s, part, 0:h, :] = out[s, part, 0:h, :] + land_r[s, 1, part].astype(F32)
-            out[s, part, :, h:] = out[s, part, :, h:] + land_c[s, 0, part].astype(F32)
-            out[s, part, :, 0:h] = out[s, part, :, 0:h] + land_c[s, 1, part].astype(F32)
-            for d, rows in ((0, pl.ds(h, h)), (1, pl.ds(0, h))):
-                place = (s, part, rows, blk(core))
-                out[place] = out[place] + land_d[s, d, part].astype(F32)
+        whole, first, second = pl.ds(0, n), pl.ds(0, h), pl.ds(h, h)
+        for ds, landed, rows, cols in (
+            ((4,), land_c.at[s, 0], whole, second),
+            ((5,), land_c.at[s, 1], whole, first),
+            ((6,), land_d.at[s, 0], second, blk(core)),
+            ((7,), land_d.at[s, 1], first, blk(core)),
+            ((0, 1), land_r.at[s, 0], second, whole),
+            ((2, 3), land_r.at[s, 1], first, whole),
+        ):
+
+            @pl.when(gets[ds[0]])
+            def _(ds=ds, landed=landed, rows=rows, cols=cols):
+                for d in ds:
+                    back(s, d).wait_recv()
+                for part in range(2):
+                    place = (s, part, rows, cols)
+                    out[place] = out[place] + landed[part].astype(F32)
+
         return carry
 
     lax.fori_loop(0, slices, collect, 0)
 
     def drain(s, carry):
-        for d in range(10):
-            halo(s, d).wait_send()
-            back(s, d).wait_send()
+        await_departure(halo, s, range(10))
+        await_departure(back, s, range(10))
         return carry
 
     lax.fori_loop(0, slices, drain, 0)

time: 93.3 us -> 88.4 us (0.947)
  the two profiles are of different devices: /device:TPU:1 before, /device:TPU:43 now
where the time goes in v3:
time: 88.4 us; the launch traced here: 87.1 us
  Pallas kernels  85.7 us (97%)
  local copies, waits for them, and re-layouts  1.32 us (1%)
    pallas_call x1, Pallas kernels, per_device(): pl.pallas_call(functools.partial(kernel, grid), out_shape=pltpu.VMEM(obje...  85.7 us

profile of v3, /device:TPU:43, one launch (start us, length us, event | category | flops | bytes accessed | tf_op | source)
XLA Modules:
  0.0 87.1 jit_solution(5011306959766594072)
XLA Ops:
  0.0 85.7 %shard_map.73 = f32[4,2,256,256]{3,2,1,0:T(8,128)S(1)} custom-call(s32[2,3]{1,0:T(2,128)} %bitcast.1, s32[3]{0:T(128)} %live.1, bf16[4,2,256,256]{3,2,1,0:T(8,128)(2,1)} %obj.1, f32[2,256,256]{2,1,0:T(8,128)} %probe_in.1, f32[3,256,256]{2,1,0:T(8,128)} %inten_in.1, f32[256,256]{1,0:T(8,128)} %phase_in.1, f32[2,256,256]{2,1,0:T(8,128)} %constant.2.clone.dft_in), custom_call_target="tpu_custom_call" | custom-call | tf_op jit(solution)/shard_map/pallas_call | solution.py:469
  85.7 1.3 %copy.9 = f32[4,2,256,256]{3,2,1,0:T(8,128)} copy(f32[4,2,256,256]{3,2,1,0:T(8,128)S(1)} %shard_map.73) | data formatting | bytes 4194304

commit v4 on v3

--- a/solution.py
+++ b/solution.py
@@ -65,6 +65,10 @@
     grad_send,
     grad_recv,
     own_sem,
+    stage,
+    first_send,
+    first_recv,
+    second_send,
 ):
     nty, ntx = grid
     slices, _, n, _ = obj.shape
@@ -115,9 +119,28 @@
         has_down,
     )
 
+    odd = lax.rem(ty, 2)
+    partner = ty + 1 - 2 * odd
+    last = slices - 1
+
+    def diverted(row):
+        rings = jnp.where(lax.rem(row, 2) == 0, row, nty - 1 - row) // 2
+        return slices * rings // (nty // 2)
+
+    mine, theirs = diverted(ty), diverted(partner)
+    final = jnp.clip(ty + 2 - 4 * odd, 0, nty - 1)
+    behind = jnp.clip(ty - 2 + 4 * odd, 0, nty - 1)
+    served = (behind != ty) & (lax.rem(behind, 2) == odd) & (diverted((ty + behind) // 2) > 0)
+
+    def goes(way, s, d):
+        order = s if way is halo else last - s
+        if d < 4:
+            return sends[d] & ((odd == (1 if d < 2 else 0)) | (order >= mine))
+        return sends[d]
+
     def start(way, s, ds):
         for d in ds:
-            pl.when(sends[d])(way(s, d).start)
+            pl.when(goes(way, s, d))(way(s, d).start)
 
     def await_arrival(way, s, ds):
         for d in ds:
@@ -125,7 +148,7 @@
 
     def await_departure(way, s, ds):
         for d in ds:
-            pl.when(sends[d])(way(s, d).wait_send)
+            pl.when(goes(way, s, d))(way(s, d).wait_send)
 
     low, mid, high = pl.ds(0, h), pl.ds(h, n), pl.ds(3 * h, h)
 
@@ -176,6 +199,47 @@
         )[d]
         return remote(src, dst, grad_send.at[s, d], grad_recv.at[s, d], targets[d])
 
+    def to_partner(way, s):
+        src, phase_index = (obj.at[s, :, blk(odd), :], 0) if way is halo else (gpad.at[s, :, blk(3 * odd), mid], 1)
+        return remote(
+            src,
+            stage.at[phase_index, s],
+            first_send.at[phase_index, s],
+            first_recv.at[phase_index, s],
+            (partner, tx),
+        )
+
+    def to_final(way, s, e):
+        half = (1 - core, core)[e]
+        d = 2 * (1 - odd) + e
+        if way is halo:
+            dst, arrival, phase_index = pad.at[s, :, blk(3 * odd), blk(1 + half)], halo_recv.at[s, d], 0
+        else:
+            dst, arrival, phase_index = land_r.at[s, 1 - odd, :, :, blk(half)], grad_recv.at[s, d], 1
+        return remote(
+            stage.at[phase_index, s, :, :, blk(half)], dst, second_send.at[phase_index, s, e], arrival, (final, tx)
+        )
+
+    def divert(way, s):
+        pl.when((s if way is halo else last - s) < mine)(to_partner(way, s).start)
+
+    def relay(way, s):
+        @pl.when((s if way is halo else last - s) < theirs)
+        def _():
+            to_partner(way, s).wait_recv()
+            for e in range(2):
+                to_final(way, s, e).start()
+
+    def settle(way, s):
+        await_departure(way, s, range(10))
+        order = s if way is halo else last - s
+        pl.when(order < mine)(to_partner(way, s).wait_send)
+
+        @pl.when(order < theirs)
+        def _():
+            for e in range(2):
+                to_final(way, s, e).wait_send()
+
     own = [
         pltpu.make_async_copy(src, dst, own_sem.at[index])
         for index, (src, dst) in enumerate(
@@ -190,12 +254,19 @@
         def _(d=d):
             pl.semaphore_signal(barrier, inc=1, device_id=targets[d], device_id_type=MESH)
 
-    pl.semaphore_wait(barrier, sum(sends[d].astype(jnp.int32) for d in (0, 2, 4, 5, 6, 7)))
-
-    for s in range(slices):
-        start(halo, s, (4, 5))
-    for s in range(slices):
-        start(halo, s, (6, 7, 0, 2, 1, 3))
+    @pl.when(served)
+    def _():
+        pl.semaphore_signal(barrier, inc=1, device_id=(behind, tx), device_id_type=MESH)
+
+    expected = [sends[d] for d in (0, 2, 4, 5, 6, 7)] + [theirs > 0]
+    pl.semaphore_wait(barrier, sum(there.astype(jnp.int32) for there in expected))
+
+    def ask(s):
+        start(halo, s, (4, 5, 6, 7))
+        divert(halo, s)
+        start(halo, s, (0, 2, 1, 3))
+
+    ask(0)
     for copy in own:
         copy.start()
 
@@ -236,6 +307,7 @@
         return carry
 
     lax.fori_loop(0, slots, prepare, 0)
+    ask(1)
     for copy in own[3:]:
         copy.wait()
 
@@ -315,9 +387,13 @@
             stage(k, *operands)
 
     def arrive(s):
+        relay(halo, s)
         await_arrival(halo, s, (0, 2))
         start(halo, s, (8, 9))
-        await_arrival(halo, s, (1, 3, 4, 5, 6, 7, 8, 9))
+        await_arrival(halo, s, (1, 3, 4, 5, 6, 7))
+        if not isinstance(s, int):
+            pl.when(s + 2 < slices)(lambda: ask(s + 2))
+        await_arrival(halo, s, (8, 9))
 
     def forward(s, carry):
         arrive(s)
@@ -332,7 +408,6 @@
             wave[k, s + 1] = dot(mb[k], tre[k])
         return carry
 
-    last = slices - 1
     lax.fori_loop(0, last, forward, 0)
     arrive(last)
 
@@ -346,7 +421,9 @@
                     place = (s, part, rows, blk(2 - core))
                     total = gpad[place].astype(F32) + land_m[s, d, part].astype(F32)
                     gpad[place] = total.astype(BF16)
-                back(s, 2 * d).start()
+                start(back, s, (2 * d,))
+
+        divert(back, s)
 
     def combine(s):
         for part in range(2):
@@ -380,10 +457,6 @@
     def sides(s):
         start(back, s, (8, 9, 4, 5, 6, 7))
 
-    def rows_out(s):
-        start(back, s, (1, 3))
-        tops(s)
-
     for k in range(slots):
         illuminate(last, k)
     every(left_of, tl)
@@ -399,20 +472,13 @@
             gradient(s, k, True)
         combine(s)
         sides(s)
-
-        @pl.when(t > 1)
+        start(back, s, (1, 3))
+        every(right_adjoint, tr)
+        tops(s)
+
+        @pl.when(t > 0)
         def _():
-            rows_out(s + 1)
-
-        @pl.when(t == 0)
-        def _():
-            start(back, s, (1, 3))
-
-        every(right_adjoint, tr)
-
-        @pl.when(t == 0)
-        def _():
-            tops(s)
+            relay(back, s + 1)
 
         every(left_adjoint, tl)
         every(propagate_adjoint)
@@ -425,8 +491,9 @@
         gradient(0, k, False)
     combine(0)
     sides(0)
-    rows_out(1)
-    rows_out(0)
+    start(back, 0, (1, 3))
+    relay(back, 1)
+    tops(0)
 
     def collect(t, carry):
         s = last - t
@@ -453,8 +520,8 @@
     lax.fori_loop(0, slices, collect, 0)
 
     def drain(s, carry):
-        await_departure(halo, s, range(10))
-        await_departure(back, s, range(10))
+        settle(halo, s)
+        settle(back, s)
         return carry
 
     lax.fori_loop(0, slices, drain, 0)
@@ -501,6 +568,10 @@
             pltpu.SemaphoreType.DMA((slices, 10)),
             pltpu.SemaphoreType.DMA((slices, 10)),
             pltpu.SemaphoreType.DMA((5,)),
+            pltpu.VMEM((2, slices, 2, h, n), BF16),
+            pltpu.SemaphoreType.DMA((2, slices)),
+            pltpu.SemaphoreType.DMA((2, slices)),
+            pltpu.SemaphoreType.DMA((2, slices, 2)),
         ],
         compiler_params=pltpu.CompilerParams(
             collective_id=0, has_side_effects=True, vmem_limit_bytes=56 * 1024 * 1024

time: 88.4 us -> 84.6 us (0.957)
  Pallas kernels: 85.7 us -> 82.5 us
    pallas_call x1, Pallas kernels: 85.7 us -> 82.5 us  [per_device(): pl.pallas_call(functools.partial(kernel, grid), out_shape=pltpu.VMEM(obje...]
where the time goes in v4:
time: 84.6 us; the launch traced here: 83.9 us
  Pallas kernels  82.5 us (98%)
  local copies, waits for them, and re-layouts  1.32 us (2%)
    pallas_call x1, Pallas kernels, per_device(): pl.pallas_call(functools.partial(kernel, grid), out_shape=pltpu.VMEM(obje...  82.5 us

profile of v4, /device:TPU:43, one launch (start us, length us, event | category | flops | bytes accessed | tf_op | source)
XLA Modules:
  0.0 83.9 jit_solution(11467529993348533578)
XLA Ops:
  0.0 82.5 %shard_map.73 = f32[4,2,256,256]{3,2,1,0:T(8,128)S(1)} custom-call(s32[2,3]{1,0:T(2,128)} %bitcast.1, s32[3]{0:T(128)} %live.1, bf16[4,2,256,256]{3,2,1,0:T(8,128)(2,1)} %obj.1, f32[2,256,256]{2,1,0:T(8,128)} %probe_in.1, f32[3,256,256]{2,1,0:T(8,128)} %inten_in.1, f32[256,256]{1,0:T(8,128)} %phase_in.1, f32[2,256,256]{2,1,0:T(8,128)} %constant.2.clone.dft_in), custom_call_target="tpu_custom_call" | custom-call | tf_op jit(solution)/shard_map/pallas_call | solution.py:536
  82.5 1.3 %copy.9 = f32[4,2,256,256]{3,2,1,0:T(8,128)} copy(f32[4,2,256,256]{3,2,1,0:T(8,128)S(1)} %shard_map.73) | data formatting | bytes 4194304

commit v5 on v4

--- a/solution.py
+++ b/solution.py
@@ -12,7 +12,7 @@
 MESH = pl.DeviceIdType.MESH
 BF16 = jnp.bfloat16
 F32 = jnp.float32
-ROWS = 32
+ROWS = 64
 
 
 def dft_matrix(side):

time: 84.6 us -> 84.6 us (level)
  no operation moved by 1% of the time
where the time goes in v5:
time: 84.6 us; the launch traced here: 83.9 us
  Pallas kernels  82.5 us (98%)
  local copies, waits for them, and re-layouts  1.32 us (2%)
    pallas_call x1, Pallas kernels, per_device(): pl.pallas_call(functools.partial(kernel, grid), out_shape=pltpu.VMEM(obje...  82.5 us

profile of v5, /device:TPU:43, one launch (start us, length us, event | category | flops | bytes accessed | tf_op | source)
XLA Modules:
  0.0 83.9 jit_solution(13814507147015312709)
XLA Ops:
  0.0 82.5 %shard_map.73 = f32[4,2,256,256]{3,2,1,0:T(8,128)S(1)} custom-call(s32[2,3]{1,0:T(2,128)} %bitcast.1, s32[3]{0:T(128)} %live.1, bf16[4,2,256,256]{3,2,1,0:T(8,128)(2,1)} %obj.1, f32[2,256,256]{2,1,0:T(8,128)} %probe_in.1, f32[3,256,256]{2,1,0:T(8,128)} %inten_in.1, f32[256,256]{1,0:T(8,128)} %phase_in.1, f32[2,256,256]{2,1,0:T(8,128)} %constant.2.clone.dft_in), custom_call_target="tpu_custom_call" | custom-call | tf_op jit(solution)/shard_map/pallas_call | solution.py:536
  82.5 1.3 %copy.9 = f32[4,2,256,256]{3,2,1,0:T(8,128)} copy(f32[4,2,256,256]{3,2,1,0:T(8,128)S(1)} %shard_map.73) | data formatting | bytes 4194304
